TPU v7x, 512 devices: a whole 4x4x16 slice. The times are simulated.
512 devices in a mesh: dp: 4 (over y), row: 8 (over z_lo, core), col: 16 (over z_hi, x).
Axes of the slice: x: 4, y: 4, z: 16 (z_hi: 4, z_lo: 4; z = z_hi * 4 + z_lo), core: 2. Of those that a mesh axis runs over, the one named last changes fastest.
Arguments:
- gradient_partials: bfloat16 [4, 4, 1024, 16384], P('dp', None, 'row', 'col'), may hold values from -405 to 405
- master: float32 [4, 1024, 16384], P('dp', 'row', 'col'), may hold values from -0.03 to 0.03
- row_moment: float32 [4, 1024], P('dp', 'row'), may hold values from 0.5 to 50
- col_moment: float32 [16384], P('col'), may hold values from 0.5 to 50
- amax_history: float32 [16], replicated, may hold values from 0.03 to 0.08
Outputs:
- new_master: float32 [4, 1024, 16384], P('dp', 'row', 'col')
- update: float32 [4, 1024, 16384], P('dp', 'row', 'col')
- row_new: float32 [4, 1024], P('dp', 'row')
- col_new: float32 [16384], P('col')
- codes: bfloat16 [4, 1024, 16384], P(None, 'row', 'col')
- new_history: float32 [16], replicated
- row_mean: float32 [], replicated
All inputs are finite; a program needn't handle non-finite values.
Results may differ from a plain program's by a relative error of at most 0.012.
Values may be sent and summed in bfloat16 or wider, within the bound.
A program may use at most 64 MiB of HBM per device.

v0:
```python
import jax
import jax.numpy as jnp
from jax import lax
from jax.sharding import PartitionSpec as P

D_WIN = 4096
FF_WIN = 16384


decay_rate = 0.9
epsilon = 1e-30
learn_rate = 0.01
clip_limit = 1.0
code_limit = 4.0


def moment_update(
    gradient, master, row_prev, col_prev, sum_rows, sum_cols, total_rows, total_all, largest_all
):
    square = gradient * gradient + epsilon
    row_new = (
        decay_rate * row_prev + (1.0 - decay_rate) * sum_rows(jnp.sum(square, axis=2)) / FF_WIN
    )
    col_new = (
        decay_rate * col_prev + (1.0 - decay_rate) * sum_cols(jnp.sum(square, axis=(0, 1))) / D_WIN
    )
    row_mean = total_rows(jnp.sum(row_new)) / D_WIN
    denominator = jnp.sqrt(row_new[:, :, None] * col_new[None, None, :] / row_mean)
    raw_step = gradient / denominator
    step_rms = jnp.sqrt(total_all(jnp.sum(raw_step * raw_step)) / (D_WIN * FF_WIN))
    update = raw_step / jnp.maximum(1.0, step_rms / clip_limit)
    new_master = master - learn_rate * update
    newest = largest_all(jnp.max(jnp.abs(new_master)))
    return (new_master, update, row_new, col_new, newest, row_mean)


def encode(new_master, history):
    scale = code_limit / jnp.max(history)
    return jnp.clip(new_master * scale, -code_limit, code_limit).astype(jnp.bfloat16)


def shift_history(history, newest):
    return jnp.concatenate([history[1:], newest.reshape(1)])


def body(gradient_partials, master, row_moment, col_moment, amax_history):
    partial_terms = gradient_partials.astype(jnp.float32)
    summed = lax.psum_scatter(
        partial_terms.astype(jnp.bfloat16), "dp", scatter_dimension=1, tiled=True
    ).astype(jnp.float32)[0]

    def rows_over_cols(values):
        return lax.psum(values, "col")

    def cols_over_rows(values):
        return lax.psum(values, ("dp", "row"))

    def total_of_rows(values):
        return lax.psum(values, ("dp", "row"))

    def total_of_all(values):
        return lax.psum(values, ("dp", "row", "col"))

    def largest_of_all(values):
        return lax.pmax(values, ("dp", "row", "col"))

    new_master, update, row_new, col_new, newest, row_mean = moment_update(
        summed,
        master,
        row_moment,
        col_moment,
        rows_over_cols,
        cols_over_rows,
        total_of_rows,
        total_of_all,
        largest_of_all,
    )
    codes = lax.all_gather(encode(new_master, amax_history), "dp", axis=0, tiled=True)
    return (
        new_master,
        update,
        row_new,
        col_new,
        codes,
        shift_history(amax_history, newest),
        row_mean,
    )


def solution(mesh):
    placed = (P("dp", None, "row", "col"), P("dp", "row", "col"), P("dp", "row"), P("col"), P())
    return jax.shard_map(
        body,
        mesh=mesh,
        in_specs=placed,
        out_specs=(
            P("dp", "row", "col"),
            P("dp", "row", "col"),
            P("dp", "row"),
            P("col"),
            P(None, "row", "col"),
            P(),
            P(),
        ),
        check_vma=False,
    )
```

profile of v0, /device:TPU:1, one launch (start us, length us, event | category | flops | bytes accessed | tf_op | source)
XLA Modules:
  0.0 390.0 jit_solution(5641043657053056748)
XLA Ops:
  7.2 0.0 copy-start.7
  7.2 0.0 reduce-scatter.2.cloned.1.call-start
  7.2 0.0 copy-start.2
  7.2 0.7 reduce-scatter.2.cloned.1.call-update
  7.9 0.0 all-gather.2.cloned.1.call-start
  8.0 0.0 copy-done.7
  8.0 0.6 reduce_max.18
  8.6 37.4 %reduce-scatter.2.cloned.1.call-done = bf16[1,1,128,1024]{3,2,1,0:T(8,128)(2,1)} async-done(((bf16[1,4,128,1024]{3,2,1,0:T(8,128)(2,1)}), bf16[1,1,128,1024]{3,2,1,0:T(8,128)(2,1)}) %reduce-scatter.2.cloned.1.call-update) | async-done | bytes 262160 | tf_op jit(solution)/shard_map/reduce_scatter | solution.py:48
  46.0 0.0 copy-start
  46.0 1.2 fusion.1
  47.2 47.7 %psum.28 = f32[1,128]{1,0:T(1,128)S(1)} all-reduce(f32[1,128]{1,0:T(1,128)S(1)} %bitcast.15), channel_id=1, replica_groups=mesh['dp'=4,'row'=8,'col'=16] {'col'}, use_global_device_ids=true, to_apply=%region_2.0 | all-reduce | flops 128 | bytes 1024 | tf_op jit(solution)/shard_map/psum | solution.py:53
  94.9 0.0 copy-done.6
  94.9 0.6 fusion.3
  95.5 0.0 copy-start.4
  95.5 77.5 %all-reduce = (f32[]{:T(128)}, f32[1024]{0:T(1024)S(1)}) all-reduce(f32[]{:T(128)} %get-tuple-element.14, f32[1024]{0:T(1024)S(1)} %get-tuple-element.7), channel_id=1, replica_groups=mesh['dp'=4,'row'=8,'col'=16] {'dp','row'}, use_global_device_ids=true, to_apply=%region_6.0 | all-reduce | flops 1025 | bytes 8200 | tf_op jit(solution)/shard_map/psum | solution.py:59
  173.7 0.0 copy-done.5
  173.8 0.0 copy-start.3
  173.8 0.0 copy-done
  173.8 0.9 multiply_reduce_fusion
  175.3 98.9 %psum.31 = f32[]{:T(128)} all-reduce(f32[]{:T(128)} %multiply_reduce_fusion), channel_id=1, replica_groups=mesh['dp'=4,'row'=8,'col'=16] {'dp','row','col'}, use_global_device_ids=true, to_apply=%region_8.0 | all-reduce | flops 1 | bytes 8 | tf_op jit(solution)/shard_map/psum | solution.py:62
  274.9 0.0 copy-done.4
  274.9 0.0 copy-done.3
  274.9 0.0 copy-done.2
  275.0 1.6 abs_reduce_fusion
  276.6 0.0 copy-start.1
  276.6 0.8 clamp_convert_fusion
  277.4 0.0 all-gather.2.cloned.1.call-update
  277.4 0.0 copy-done.1
  277.4 0.1 slice.3
  277.5 100.9 %pmax.7 = f32[1]{0:T(128)} all-reduce(f32[1]{0:T(128)} %bitcast.4), channel_id=1, replica_groups=mesh['dp'=4,'row'=8,'col'=16] {'dp','row','col'}, use_global_device_ids=true, to_apply=%region_11.0 | all-reduce | flops 1 | bytes 8 | tf_op jit(solution)/shard_map/pmax | solution.py:65
  378.4 1.3 pad_maximum_fusion
  379.7 2.3 copy.13
  (4 shorter events, 0.0 us)
Async XLA Ops:
  7.2 0.8 copy-start.7
  7.2 38.8 %reduce-scatter.2.cloned.1.call-start = ((), (), s32[]{:S(2)}) async-start(), calls=%async_computation.1 | async-start | bytes 1310720 | tf_op jit(solution)/shard_map/reduce_scatter | solution.py:48
  7.2 267.7 %copy-start.2 = (f32[1,128,1024]{2,1,0:T(8,128)S(1)}, f32[1,128,1024]{2,1,0:T(8,128)}, u32[]{:S(2)}) copy-start(f32[1,128,1024]{2,1,0:T(8,128)} %param.6) | copy-start | bytes 1572868
  7.9 371.8 %all-gather.2.cloned.1.call-start = ((), (), s32[]{:S(2)}) async-start(), calls=%async_computation.2 | async-start | bytes 1310720 | tf_op jit(solution)/shard_map/all_gather | solution.py:78
  46.0 127.8 %copy-start = (bf16[1,1,128,1024]{3,2,1,0:T(8,128)(2,1)S(1)}, bf16[1,1,128,1024]{3,2,1,0:T(8,128)(2,1)}, u32[]{:S(2)}) copy-start(bf16[1,1,128,1024]{3,2,1,0:T(8,128)(2,1)} %reduce-scatter.2.cloned.1.call-done) | copy-start | bytes 786436
  47.2 47.7 %copy-start.6 = (f32[1,128]{1,0:T(1,128)S(1)}, f32[1,128]{1,0:T(1,128)}, u32[]{:S(2)}) copy-start(f32[1,128]{1,0:T(1,128)} %param.7) | copy-start | bytes 1540
  95.5 179.4 %copy-start.4 = (f32[1,128]{1,0:T(1,128)}, f32[1,128]{1,0:T(1,128)S(1)}, u32[]{:S(2)}) copy-start(f32[1,128]{1,0:T(1,128)S(1)} %get-tuple-element.25) | copy-start | bytes 1540
  95.5 78.2 %copy-start.5 = (f32[1024]{0:T(1024)S(1)}, f32[1024]{0:T(1024)}, u32[]{:S(2)}) copy-start(f32[1024]{0:T(1024)} %param.8) | copy-start | bytes 12292
  173.8 101.2 %copy-start.3 = (f32[1024]{0:T(1024)}, f32[1024]{0:T(1024)S(1)}, u32[]{:S(2)}) copy-start(f32[1024]{0:T(1024)S(1)} %multiply_add_fusion) | copy-start | bytes 12292
  276.6 0.9 copy-start.1
Sparse Core Ops, SparseCore 0:
  10.8 35.1 reduce-scatter.1
  277.5 24.2 all-gather.1
where the time goes:
time: 391 us; the launch traced here: 390 us
  blocking collectives  325 us (83%)
  waiting for transfers between devices  38.1 us (10%)
  between operations  17.3 us (4%)
  other arithmetic  6.97 us (2%)
    pmax x1, blocking collectives, largest_of_all(): return lax.pmax(values, ('dp', 'row', 'col'))  101 us
    psum x1, blocking collectives, total_of_all(): return lax.psum(values, ('dp', 'row', 'col'))  98.9 us
    psum x1, blocking collectives, total_of_rows(): return lax.psum(values, ('dp', 'row'))  77.5 us
    psum x1, blocking collectives, rows_over_cols(): return lax.psum(values, 'col')  47.7 us
    reduce_scatter x1, waiting for transfers between devices, body(): lax.psum_scatter(partial_terms.astype(jnp.bfloat16), 'dp', scatter_dimens...  37.4 us
  transfers between devices with their start and end apart: 2, of which 1 were waited for; matrix products, arithmetic and copies ran while one was open for 0% of the time, Pallas kernels for 0%

commit v1 on v0

v1 whole, which is shorter than its diff:
```python
import functools

import jax
import jax.numpy as jnp
from jax import lax
from jax.experimental import pallas as pl
from jax.experimental.pallas import tpu as pltpu
from jax.sharding import PartitionSpec as P

MESH = pl.DeviceIdType.MESH
F32 = jnp.float32

decay_rate = 0.9
epsilon = 1e-30
learn_rate = 0.01
clip_limit = 1.0
code_limit = 4.0

ROWS, COLS = 128, 1024
HALF = ROWS // 2
CHUNK = 32
TILES = COLS // 128


def whole_wait(view, sem):
    pltpu.make_async_copy(view, view, sem).wait()


def step_kernel(
    sizes, grad, master, row_prev, col_prev, history,
    nm_out, up_out, codes_out, small_out,
    merge_r, merge_l, from_l, from_r, own, next_own, prev_own, sum_r, sum_l,
    g_buf, m_buf, nm_buf, up_buf, code_buf, rowp, rm_buf, cm_buf,
    core_c, yz_c, xz_r, xz_t, core_s, yz_s, xz_m, core_m, yz_m,
    rs_send, rs_recv, loc, core_send, core_recv, grp_send, grp_recv, ag_send, ag_recv,
):
    n_dp, n_row, n_col = sizes
    n_zl = n_row // 2
    n_yz = n_dp * n_zl
    total_rows, total_cols = n_dp * n_row * ROWS, n_col * COLS
    d, r, c = lax.axis_index("dp"), lax.axis_index("row"), lax.axis_index("col")
    zl, core = r // 2, r % 2
    q = d * n_zl + zl
    dn, dp_, do = lax.rem(d + 1, n_dp), lax.rem(d + n_dp - 1, n_dp), lax.rem(d + 2, n_dp)
    right, left = (dn, r, c), (dp_, r, c)
    mate = (d, zl * 2 + (1 - core), c)
    yz_peers = []
    for k in range(1, n_yz):
        p = lax.rem(q + k, n_yz)
        yz_peers.append((p // n_zl, (p % n_zl) * 2 + core, c))
    xz_peers = [(d, r, lax.rem(c + k, n_col)) for k in range(1, n_col)]
    contacts = [*yz_peers, mate, *xz_peers]

    def remote(src, dst, send, recv, to):
        return pltpu.make_async_remote_copy(
            src, dst, send, recv, device_id=to, device_id_type=MESH
        )

    loads = [
        pltpu.make_async_copy(grad.at[0, d], own, loc.at[0]),
        pltpu.make_async_copy(grad.at[0, dn, pl.ds(0, HALF)], next_own, loc.at[1]),
        pltpu.make_async_copy(grad.at[0, dp_, pl.ds(HALF, HALF)], prev_own, loc.at[2]),
        pltpu.make_async_copy(master.at[0], m_buf, loc.at[3]),
        pltpu.make_async_copy(row_prev, rm_buf, loc.at[4]),
        pltpu.make_async_copy(col_prev, cm_buf, loc.at[5]),
    ]

    barrier = pltpu.get_barrier_semaphore()
    for p in contacts:
        pl.semaphore_signal(barrier, inc=1, device_id=p, device_id_type=MESH)
    for cp in loads:
        cp.start()
    pl.semaphore_wait(barrier, len(contacts))

    n_half = HALF // CHUNK
    sends = []
    first = []
    for i in range(n_half):
        lo, hi = pl.ds(CHUNK * i, CHUNK), pl.ds(HALF + CHUNK * i, CHUNK)
        here = pl.ds(CHUNK * i, CHUNK)
        a = remote(grad.at[0, do, lo], merge_r.at[here], rs_send.at[i], rs_recv.at[i], right)
        b = remote(grad.at[0, do, hi], merge_l.at[here], rs_send.at[2 + i], rs_recv.at[2 + i], left)
        a.start()
        b.start()
        first.append((a, b))
    plain_r = remote(
        grad.at[0, dn, pl.ds(HALF, HALF)], from_l.at[pl.ds(HALF, HALF)], rs_send.at[4], rs_recv.at[4], right
    )
    plain_l = remote(
        grad.at[0, dp_, pl.ds(0, HALF)], from_r.at[pl.ds(0, HALF)], rs_send.at[5], rs_recv.at[5], left
    )
    plain_r.start()
    plain_l.start()
    loads[1].wait()
    loads[2].wait()
    merged = []
    for i in range(n_half):
        here, hi = pl.ds(CHUNK * i, CHUNK), pl.ds(HALF + CHUNK * i, CHUNK)
        a, b = first[i]
        a.wait_recv()
        sum_r[here] = (next_own[here].astype(F32) + merge_r[here].astype(F32)).astype(jnp.bfloat16)
        m = remote(sum_r.at[here], from_l.at[here], rs_send.at[6 + i], rs_recv.at[6 + i], right)
        m.start()
        b.wait_recv()
        sum_l[here] = (prev_own[here].astype(F32) + merge_l[here].astype(F32)).astype(jnp.bfloat16)
        n = remote(sum_l.at[here], from_r.at[hi], rs_send.at[8 + i], rs_recv.at[8 + i], left)
        n.start()
        merged.append((m, n))

    loads[0].wait()
    plain_r.wait_recv()
    plain_l.wait_recv()
    col_sum = jnp.zeros((8, COLS), F32)
    for i in range(n_half):
        m, n = merged[i]
        for half, cp in ((0, m), (1, n)):
            cp.wait_recv()
            rows = pl.ds(HALF * half + CHUNK * i, CHUNK)
            g = own[rows].astype(F32) + from_l[rows].astype(F32) + from_r[rows].astype(F32)
            g_buf[rows] = g
            square = g * g + epsilon
            for j in range(CHUNK // 8):
                col_sum = col_sum + square[8 * j : 8 * j + 8]
            lanes = square[:, 0:128]
            for k in range(1, TILES):
                lanes = lanes + square[:, 128 * k : 128 * k + 128]
            rowp[rows] = lanes

    flat = jnp.sum(col_sum, axis=0, keepdims=True)
    packed = jnp.concatenate([flat[:, 128 * k : 128 * k + 128] for k in range(TILES)], axis=0)
    core_c[0] = packed
    core_c_copy = remote(core_c.at[0], core_c.at[1], core_send.at[0], core_recv.at[0], mate)
    core_c_copy.start()

    def group_start(buf, mine, peers, i):
        for p in peers:
            remote(buf.at[mine], buf.at[mine], grp_send.at[i], grp_recv.at[i], p).start()

    def group_wait(buf, peers, i):
        whole_wait(buf.at[pl.ds(0, len(peers))], grp_recv.at[i])

    def group_done(buf, peers, i):
        whole_wait(buf.at[pl.ds(0, len(peers))], grp_send.at[i])

    def add_all(buf, n):
        total = buf[0]
        for k in range(1, n):
            total = total + buf[k]
        return total

    def lanes_to_row(values):
        return jnp.sum(values.T, axis=0, keepdims=True)

    def row_to_lanes(values):
        return jnp.broadcast_to(values, (128, 128)).T

    xz_r[c] = lanes_to_row(rowp[...])
    group_start(xz_r, c, xz_peers, 0)
    core_c_copy.wait_recv()
    yz_c[q] = core_c[0] + core_c[1]
    group_start(yz_c, q, yz_peers, 1)
    loads[4].wait()
    loads[5].wait()
    group_wait(yz_c, yz_peers, 1)
    col_total = add_all(yz_c, n_yz)
    col_old = jnp.concatenate(
        [cm_buf[pl.ds(128 * k, 128)].reshape(1, 128) for k in range(TILES)], axis=0
    )
    col_new = decay_rate * col_old + (1.0 - decay_rate) * (col_total / total_rows)
    small_out[0:8] = col_new
    inv_col = 1.0 / col_new
    root_col = 1.0 / jnp.sqrt(col_new)

    lanes = jnp.zeros((ROWS, 128), F32)
    for k in range(TILES):
        g = g_buf[:, pl.ds(128 * k, 128)]
        lanes = lanes + g * g * inv_col[k : k + 1]
    xz_t[c] = lanes_to_row(lanes)
    group_start(xz_t, c, xz_peers, 2)
    group_wait(xz_r, xz_peers, 0)
    row_total = add_all(xz_r, n_col)
    row_new = decay_rate * rm_buf[...] + (1.0 - decay_rate) * (row_total / total_cols)
    small_out[8:9] = row_new
    row_factor = row_to_lanes(1.0 / jnp.sqrt(row_new))
    group_wait(xz_t, xz_peers, 2)
    weighted = add_all(xz_t, n_col) / row_new

    core_s[0] = jnp.concatenate([weighted, row_new], axis=0)
    core_s_copy = remote(core_s.at[0], core_s.at[1], core_send.at[1], core_recv.at[1], mate)
    core_s_copy.start()
    core_s_copy.wait_recv()
    yz_s[q] = core_s[0] + core_s[1]
    group_start(yz_s, q, yz_peers, 3)
    largest_old = history[0]
    for i in range(1, 16):
        largest_old = jnp.maximum(largest_old, history[i])
    scale = code_limit / jnp.full((1, 128), largest_old, F32)
    loads[3].wait()
    group_wait(yz_s, yz_peers, 3)
    totals = jnp.sum(add_all(yz_s, n_yz), axis=1, keepdims=True)
    row_mean = totals[1:2] / total_rows
    step_rms = jnp.sqrt(row_mean * totals[0:1] / (float(total_rows) * float(total_cols)))
    factor = jnp.sqrt(row_mean) / jnp.maximum(1.0, step_rms / clip_limit)
    small_out[10:11] = jnp.broadcast_to(row_mean, (1, 128))
    row_factor = row_factor * factor

    largest = jnp.zeros((ROWS, 128), F32)
    for k in range(TILES):
        cols = pl.ds(128 * k, 128)
        update = g_buf[:, cols] * row_factor * root_col[k : k + 1]
        new_master = m_buf[:, cols] - learn_rate * update
        up_buf[:, cols] = update
        nm_buf[:, cols] = new_master
        code_buf[:, cols] = jnp.clip(new_master * scale, -code_limit, code_limit).astype(jnp.bfloat16)
        largest = jnp.maximum(largest, jnp.abs(new_master))
    xz_m[c] = jnp.max(largest, axis=0, keepdims=True)
    group_start(xz_m, c, xz_peers, 4)

    top, bottom = pl.ds(0, HALF), pl.ds(HALF, HALF)
    to_right = [
        remote(code_buf.at[part], codes_out.at[d, part], ag_send.at[i], ag_recv.at[i], right)
        for i, part in enumerate((top, bottom))
    ]
    to_left = [
        remote(code_buf.at[part], codes_out.at[d, part], ag_send.at[2 + i], ag_recv.at[2 + i], left)
        for i, part in enumerate((bottom, top))
    ]
    for i in range(2):
        to_right[i].start()
        to_left[i].start()
    stores = [
        pltpu.make_async_copy(code_buf, codes_out.at[d], loc.at[6]),
        pltpu.make_async_copy(nm_buf, nm_out, loc.at[7]),
        pltpu.make_async_copy(up_buf, up_out, loc.at[8]),
    ]
    for cp in stores:
        cp.start()
    to_right[0].wait_recv()
    on_right = remote(
        codes_out.at[dp_, top], codes_out.at[dp_, top], ag_send.at[4], ag_recv.at[4], right
    )
    on_right.start()
    to_left[0].wait_recv()
    on_left = remote(
        codes_out.at[dn, bottom], codes_out.at[dn, bottom], ag_send.at[5], ag_recv.at[5], left
    )
    on_left.start()

    def max_all(buf, n):
        total = buf[0]
        for k in range(1, n):
            total = jnp.maximum(total, buf[k])
        return total

    group_wait(xz_m, xz_peers, 4)
    core_m[0] = max_all(xz_m, n_col)
    core_m_copy = remote(core_m.at[0], core_m.at[1], core_send.at[2], core_recv.at[2], mate)
    core_m_copy.start()
    core_m_copy.wait_recv()
    yz_m[q] = jnp.maximum(core_m[0], core_m[1])
    group_start(yz_m, q, yz_peers, 5)

    for cp in stores:
        cp.wait()
    for a, b in first:
        a.wait_send()
        b.wait_send()
    plain_r.wait_send()
    plain_l.wait_send()
    for m, n in merged:
        m.wait_send()
        n.wait_send()
    core_c_copy.wait_send()
    core_s_copy.wait_send()
    core_m_copy.wait_send()
    group_done(xz_r, xz_peers, 0)
    group_done(yz_c, yz_peers, 1)
    group_done(xz_t, xz_peers, 2)
    group_done(yz_s, yz_peers, 3)
    group_done(xz_m, xz_peers, 4)
    to_right[1].wait_recv()
    to_left[1].wait_recv()
    on_right.wait_recv()
    on_left.wait_recv()
    group_wait(yz_m, yz_peers, 5)
    newest = jnp.max(max_all(yz_m, n_yz), axis=1, keepdims=True)
    small_out[9:10] = jnp.broadcast_to(newest, (1, 128))
    small_out[11:16] = jnp.zeros((5, 128), F32)
    for cp in (*to_right, *to_left, on_right, on_left):
        cp.wait_send()
    group_done(yz_m, yz_peers, 5)


def finish_kernel(
    nm_in, up_in, codes_in, small, history,
    nm_out, up_out, row_out, col_out, codes_out, history_out, mean_out, sems,
):
    copies = [
        pltpu.make_async_copy(codes_in, codes_out, sems.at[0]),
        pltpu.make_async_copy(nm_in, nm_out, sems.at[1]),
        pltpu.make_async_copy(up_in, up_out, sems.at[2]),
    ]
    for cp in copies:
        cp.start()
    row_out[...] = small[8:9]
    for k in range(TILES):
        col_out[pl.ds(128 * k, 128)] = small[k]
    for i in range(15):
        history_out[i] = history[i + 1]
    history_out[15] = jnp.max(small[9:10])
    mean_out[0] = jnp.max(small[10:11])
    for cp in copies:
        cp.wait()


def body(sizes, grad, master, row_prev, col_prev, history):
    n_dp, n_row, n_col = sizes
    n_yz = n_dp * n_row // 2
    bf = jnp.bfloat16
    anywhere = pl.BlockSpec(memory_space=pl.ANY)
    vmem = pl.BlockSpec(memory_space=pltpu.VMEM)
    smem = pl.BlockSpec(memory_space=pltpu.SMEM)
    block = jax.ShapeDtypeStruct((ROWS, COLS), F32)
    codes = jax.ShapeDtypeStruct((n_dp, ROWS, COLS), bf)
    V = pltpu.VMEM
    dma = pltpu.SemaphoreType.DMA
    new_master, update, coded, small = pl.pallas_call(
        functools.partial(step_kernel, sizes),
        out_shape=[block, block, codes, jax.ShapeDtypeStruct((16, 128), F32)],
        in_specs=[anywhere, anywhere, anywhere, anywhere, smem],
        out_specs=[anywhere, anywhere, anywhere, vmem],
        scratch_shapes=[
            V((HALF, COLS), bf), V((HALF, COLS), bf),
            V((ROWS, COLS), bf), V((ROWS, COLS), bf), V((ROWS, COLS), bf),
            V((HALF, COLS), bf), V((HALF, COLS), bf), V((HALF, COLS), bf), V((HALF, COLS), bf),
            V((ROWS, COLS), F32), V((ROWS, COLS), F32), V((ROWS, COLS), F32), V((ROWS, COLS), F32),
            V((ROWS, COLS), bf), V((ROWS, 128), F32), V((1, 128), F32), V((COLS,), F32),
            V((2, 8, 128), F32), V((n_yz, 8, 128), F32),
            V((n_col, 1, 128), F32), V((n_col, 1, 128), F32),
            V((2, 2, 128), F32), V((n_yz, 2, 128), F32),
            V((n_col, 1, 128), F32), V((2, 1, 128), F32), V((n_yz, 1, 128), F32),
            dma((10,)), dma((10,)), dma((9,)), dma((3,)), dma((3,)), dma((6,)), dma((6,)), dma((6,)), dma((6,)),
        ],
        compiler_params=pltpu.CompilerParams(
            collective_id=0, has_side_effects=True, vmem_limit_bytes=16 * 1024 * 1024
        ),
        name="step",
    )(grad, master, row_prev, col_prev, history)
    new_master, update, row_new, col_new, coded, new_history, row_mean = pl.pallas_call(
        finish_kernel,
        out_shape=[
            block, block, jax.ShapeDtypeStruct((1, ROWS), F32), jax.ShapeDtypeStruct((COLS,), F32), codes,
            jax.ShapeDtypeStruct((16,), F32), jax.ShapeDtypeStruct((1,), F32),
        ],
        in_specs=[anywhere, anywhere, anywhere, vmem, smem],
        out_specs=[anywhere, anywhere, vmem, vmem, anywhere, smem, smem],
        scratch_shapes=[dma((3,))],
        name="finish",
    )(new_master, update, coded, small, history)
    return (
        new_master[None], update[None], row_new, col_new, coded, new_history, row_mean.reshape(()),
    )


def solution(mesh):
    sizes = tuple(mesh.shape[a] for a in ("dp", "row", "col"))
    placed = (P("dp", None, "row", "col"), P("dp", "row", "col"), P("dp", "row"), P("col"), P())
    return jax.shard_map(
        functools.partial(body, sizes),
        mesh=mesh,
        in_specs=placed,
        out_specs=(
            P("dp", "row", "col"),
            P("dp", "row", "col"),
            P("dp", "row"),
            P("col"),
            P(None, "row", "col"),
            P(),
            P(),
        ),
        check_vma=False,
    )
```

time: 391 us -> 137 us (0.35)
  blocking collectives: 325 us -> 0 us
  Pallas kernels: 0 us -> 129 us
  waiting for transfers between devices: 38.1 us -> 0 us
  between operations: 17.3 us -> 0.67 us
  other arithmetic: 6.97 us -> 0 us
  local copies, waits for them, and re-layouts: 2.4 us -> 7.45 us
    psum x3 -> x0, blocking collectives: 224 us -> none  [the longest x1 98.9 us: total_of_all(): return lax.psum(values, ('dp', 'row', 'col'))]
    pallas_call x0 -> x2, Pallas kernels: none -> 129 us  [the longest x1 66.1 us: body(): pl.pallas_call(finish_kernel, out_shape=[block, block, jax.ShapeDtypeStru...]
    pmax x1 -> x0, blocking collectives: 101 us -> none  [largest_of_all(): return lax.pmax(values, ('dp', 'row', 'col'))]
    reduce_scatter x1 -> x0, waiting for transfers between devices: 37.4 us -> none  [body(): lax.psum_scatter(partial_terms.astype(jnp.bfloat16), 'dp', scatter_dimens...]
    unnamed x17 -> x18, local copies, waits for them, and re-layouts: 2.33 us -> 7.45 us
  transfers between devices with their start and end apart: 2 -> 0, of which waited for: 1 -> 0; matrix products, arithmetic and copies ran while one was open for 0% -> 0% of each run, Pallas kernels for 0% -> 0%
where the time goes in v1:
time: 137 us
  Pallas kernels  129 us (94%)
  local copies, waits for them, and re-layouts  7.45 us (5%)
    pallas_call x1, Pallas kernels, body(): pl.pallas_call(finish_kernel, out_shape=[block, block, jax.ShapeDtypeStru...  66.1 us
    pallas_call x1, Pallas kernels, body(): pl.pallas_call(functools.partial(step_kernel, sizes), out_shape=[block, b...  62.8 us
    unnamed x18, local copies, waits for them, and re-layouts  7.45 us

profile of v1, /device:TPU:1, one launch (start us, length us, event | category | flops | bytes accessed | tf_op | source)
XLA Modules:
  0.0 137.0 jit_solution(18164814694755699614)
XLA Ops:
  0.6 0.0 copy-start.1
  0.6 1.2 copy-done.1
  1.9 0.0 copy-start.4
  1.9 1.0 copy-done.4
  2.9 0.0 copy-start.6
  2.9 0.7 copy-done.6
  3.6 0.0 copy-start.7
  3.6 0.7 copy-done.7
  4.2 0.0 copy-start.8
  4.2 0.7 copy-done.8
  4.9 62.8 %step.1 = (f32[128,1024]{1,0:T(8,128)S(1)}, f32[128,1024]{1,0:T(8,128)S(1)}, bf16[4,128,1024]{2,1,0:T(8,128)(2,1)S(1)}, f32[16,128]{1,0:T(8,128)S(1)}) custom-call(bf16[1,4,128,1024]{3,2,1,0:T(8,128)(2,1)S(1)} %copy-done.1, f32[1,128,1024]{2,1,0:T(8,128)S(1)} %copy-done.4, f32[1,128]{1,0:T(1,128)S(1)} %copy-done.8, f32[1024]{0:T(1024)S(1)} %copy-done.6, ...), custom_call_target="tpu_custom_call" | custom-call | tf_op jit(solution)/shard_map/step/pallas_call | solution.py:327
  67.7 0.0 copy-start
  67.7 1.0 copy-done
  68.7 0.0 copy-start.2
  68.7 0.8 copy-done.2
  69.5 0.0 copy-start.3
  69.5 0.8 copy-done.3
  70.3 0.0 copy-start.5
  70.3 0.6 copy-done.5
  70.9 66.1 %finish.1 = (f32[128,1024]{1,0:T(8,128)}, f32[128,1024]{1,0:T(8,128)}, f32[1,128]{1,0:T(1,128)}, f32[1024]{0:T(1024)}, bf16[4,128,1024]{2,1,0:T(8,128)(2,1)}, /*index=5*/f32[16]{0:T(128)}, f32[1]{0:T(128)}) custom-call(f32[128,1024]{1,0:T(8,128)} %copy-done.2, f32[128,1024]{1,0:T(8,128)} %copy-done.3, bf16[4,128,1024]{2,1,0:T(8,128)(2,1)} %copy-done, ...), custom_call_target="tpu_custom_call" | custom-call | tf_op jit(solution)/shard_map/finish/pallas_call | solution.py:349
Async XLA Ops:
  0.6 1.2 copy-start.1
  1.9 1.0 copy-start.4
  2.9 0.7 copy-start.6
  3.6 0.7 copy-start.7
  4.2 0.7 copy-start.8
  67.7 1.0 copy-start
  68.7 0.8 copy-start.2
  69.5 0.8 copy-start.3
  70.3 0.6 copy-start.5

commit v2 on v1

--- a/solution.py
+++ b/solution.py
@@ -26,11 +26,15 @@
     pltpu.make_async_copy(view, view, sem).wait()
 
 
+def far_first(n):
+    return sorted(range(n), key=lambda k: -min(k, n - k))
+
+
 def step_kernel(
     sizes, grad, master, row_prev, col_prev, history,
-    nm_out, up_out, codes_out, small_out,
+    nm_out, up_out, codes_out, row_out, col_out, tail_out,
     merge_r, merge_l, from_l, from_r, own, next_own, prev_own, sum_r, sum_l,
-    g_buf, m_buf, nm_buf, up_buf, code_buf, rowp, rm_buf, cm_buf,
+    g_buf, m_buf, rowp, rm_buf, cm_buf, old,
     core_c, yz_c, xz_r, xz_t, core_s, yz_s, xz_m, core_m, yz_m,
     rs_send, rs_recv, loc, core_send, core_recv, grp_send, grp_recv, ag_send, ag_recv,
 ):
@@ -39,16 +43,26 @@
     n_yz = n_dp * n_zl
     total_rows, total_cols = n_dp * n_row * ROWS, n_col * COLS
     d, r, c = lax.axis_index("dp"), lax.axis_index("row"), lax.axis_index("col")
+    n_x = min(n_col, 4)
+    n_zh = n_col // n_x
     zl, core = r // 2, r % 2
+    zh, x = c // n_x, c % n_x
     q = d * n_zl + zl
     dn, dp_, do = lax.rem(d + 1, n_dp), lax.rem(d + n_dp - 1, n_dp), lax.rem(d + 2, n_dp)
     right, left = (dn, r, c), (dp_, r, c)
     mate = (d, zl * 2 + (1 - core), c)
-    yz_peers = []
-    for k in range(1, n_yz):
-        p = lax.rem(q + k, n_yz)
-        yz_peers.append((p // n_zl, (p % n_zl) * 2 + core, c))
-    xz_peers = [(d, r, lax.rem(c + k, n_col)) for k in range(1, n_col)]
+    yz_peers = [
+        (lax.rem(d + i, n_dp), lax.rem(zl + j, n_zl) * 2 + core, c)
+        for i in far_first(n_dp)
+        for j in far_first(n_zl)
+        if i or j
+    ]
+    xz_peers = [
+        (d, r, lax.rem(zh + i, n_zh) * n_x + lax.rem(x + j, n_x))
+        for i in far_first(n_zh)
+        for j in far_first(n_x)
+        if i or j
+    ]
     contacts = [*yz_peers, mate, *xz_peers]
 
     def remote(src, dst, send, recv, to):
@@ -63,6 +77,7 @@
         pltpu.make_async_copy(master.at[0], m_buf, loc.at[3]),
         pltpu.make_async_copy(row_prev, rm_buf, loc.at[4]),
         pltpu.make_async_copy(col_prev, cm_buf, loc.at[5]),
+        pltpu.make_async_copy(history, old, loc.at[6]),
     ]
 
     barrier = pltpu.get_barrier_semaphore()
@@ -167,7 +182,8 @@
         [cm_buf[pl.ds(128 * k, 128)].reshape(1, 128) for k in range(TILES)], axis=0
     )
     col_new = decay_rate * col_old + (1.0 - decay_rate) * (col_total / total_rows)
-    small_out[0:8] = col_new
+    for k in range(TILES):
+        col_out[pl.ds(128 * k, 128)] = col_new[k]
     inv_col = 1.0 / col_new
     root_col = 1.0 / jnp.sqrt(col_new)
 
@@ -180,7 +196,7 @@
     group_wait(xz_r, xz_peers, 0)
     row_total = add_all(xz_r, n_col)
     row_new = decay_rate * rm_buf[...] + (1.0 - decay_rate) * (row_total / total_cols)
-    small_out[8:9] = row_new
+    row_out[...] = row_new
     row_factor = row_to_lanes(1.0 / jnp.sqrt(row_new))
     group_wait(xz_t, xz_peers, 2)
     weighted = add_all(xz_t, n_col) / row_new
@@ -191,9 +207,14 @@
     core_s_copy.wait_recv()
     yz_s[q] = core_s[0] + core_s[1]
     group_start(yz_s, q, yz_peers, 3)
-    largest_old = history[0]
+    loads[6].wait()
+    largest_old = old[0]
     for i in range(1, 16):
-        largest_old = jnp.maximum(largest_old, history[i])
+        largest_old = jnp.maximum(largest_old, old[i])
+    lane = lax.broadcasted_iota(jnp.int32, (1, 128), 1)
+    shifted = jnp.zeros((1, 128), F32)
+    for i in range(15):
+        shifted = jnp.where(lane == i, old[i + 1], shifted)
     scale = code_limit / jnp.full((1, 128), largest_old, F32)
     loads[3].wait()
     group_wait(yz_s, yz_peers, 3)
@@ -201,7 +222,8 @@
     row_mean = totals[1:2] / total_rows
     step_rms = jnp.sqrt(row_mean * totals[0:1] / (float(total_rows) * float(total_cols)))
     factor = jnp.sqrt(row_mean) / jnp.maximum(1.0, step_rms / clip_limit)
-    small_out[10:11] = jnp.broadcast_to(row_mean, (1, 128))
+    tail_out[1:2] = jnp.broadcast_to(row_mean, (1, 128))
+    tail_out[2:8] = jnp.zeros((6, 128), F32)
     row_factor = row_factor * factor
 
     largest = jnp.zeros((ROWS, 128), F32)
@@ -209,32 +231,25 @@
         cols = pl.ds(128 * k, 128)
         update = g_buf[:, cols] * row_factor * root_col[k : k + 1]
         new_master = m_buf[:, cols] - learn_rate * update
-        up_buf[:, cols] = update
-        nm_buf[:, cols] = new_master
-        code_buf[:, cols] = jnp.clip(new_master * scale, -code_limit, code_limit).astype(jnp.bfloat16)
+        up_out[:, cols] = update
+        nm_out[:, cols] = new_master
+        codes_out[d, :, cols] = jnp.clip(new_master * scale, -code_limit, code_limit).astype(jnp.bfloat16)
         largest = jnp.maximum(largest, jnp.abs(new_master))
     xz_m[c] = jnp.max(largest, axis=0, keepdims=True)
     group_start(xz_m, c, xz_peers, 4)
 
     top, bottom = pl.ds(0, HALF), pl.ds(HALF, HALF)
     to_right = [
-        remote(code_buf.at[part], codes_out.at[d, part], ag_send.at[i], ag_recv.at[i], right)
+        remote(codes_out.at[d, part], codes_out.at[d, part], ag_send.at[i], ag_recv.at[i], right)
         for i, part in enumerate((top, bottom))
     ]
     to_left = [
-        remote(code_buf.at[part], codes_out.at[d, part], ag_send.at[2 + i], ag_recv.at[2 + i], left)
+        remote(codes_out.at[d, part], codes_out.at[d, part], ag_send.at[2 + i], ag_recv.at[2 + i], left)
         for i, part in enumerate((bottom, top))
     ]
     for i in range(2):
         to_right[i].start()
         to_left[i].start()
-    stores = [
-        pltpu.make_async_copy(code_buf, codes_out.at[d], loc.at[6]),
-        pltpu.make_async_copy(nm_buf, nm_out, loc.at[7]),
-        pltpu.make_async_copy(up_buf, up_out, loc.at[8]),
-    ]
-    for cp in stores:
-        cp.start()
     to_right[0].wait_recv()
     on_right = remote(
         codes_out.at[dp_, top], codes_out.at[dp_, top], ag_send.at[4], ag_recv.at[4], right
@@ -260,8 +275,6 @@
     yz_m[q] = jnp.maximum(core_m[0], core_m[1])
     group_start(yz_m, q, yz_peers, 5)
 
-    for cp in stores:
-        cp.wait()
     for a, b in first:
         a.wait_send()
         b.wait_send()
@@ -284,31 +297,36 @@
     on_left.wait_recv()
     group_wait(yz_m, yz_peers, 5)
     newest = jnp.max(max_all(yz_m, n_yz), axis=1, keepdims=True)
-    small_out[9:10] = jnp.broadcast_to(newest, (1, 128))
-    small_out[11:16] = jnp.zeros((5, 128), F32)
+    tail_out[0:1] = jnp.where(lane == 15, newest, shifted)
     for cp in (*to_right, *to_left, on_right, on_left):
         cp.wait_send()
     group_done(yz_m, yz_peers, 5)
 
 
 def finish_kernel(
-    nm_in, up_in, codes_in, small, history,
-    nm_out, up_out, row_out, col_out, codes_out, history_out, mean_out, sems,
+    nm_in, up_in, codes_in, row_in, col_in, tail,
+    nm_out, up_out, row_out, col_out, codes_out, history_out, mean_out, last, mean, sems,
 ):
     copies = [
-        pltpu.make_async_copy(codes_in, codes_out, sems.at[0]),
-        pltpu.make_async_copy(nm_in, nm_out, sems.at[1]),
-        pltpu.make_async_copy(up_in, up_out, sems.at[2]),
-    ]
-    for cp in copies:
+        pltpu.make_async_copy(a, b, sems.at[i])
+        for i, (a, b) in enumerate(
+            (
+                (codes_in, codes_out),
+                (nm_in, nm_out),
+                (up_in, up_out),
+                (row_in, row_out),
+                (col_in, col_out),
+                (last, history_out),
+                (mean, mean_out),
+            )
+        )
+    ]
+    for cp in copies[:5]:
         cp.start()
-    row_out[...] = small[8:9]
-    for k in range(TILES):
-        col_out[pl.ds(128 * k, 128)] = small[k]
-    for i in range(15):
-        history_out[i] = history[i + 1]
-    history_out[15] = jnp.max(small[9:10])
-    mean_out[0] = jnp.max(small[10:11])
+    last[...] = tail[0, 0:16]
+    mean[...] = tail[1, 0:1]
+    for cp in copies[5:]:
+        cp.start()
     for cp in copies:
         cp.wait()
 
@@ -319,44 +337,46 @@
     bf = jnp.bfloat16
     anywhere = pl.BlockSpec(memory_space=pl.ANY)
     vmem = pl.BlockSpec(memory_space=pltpu.VMEM)
-    smem = pl.BlockSpec(memory_space=pltpu.SMEM)
+    hbm = pl.BlockSpec(memory_space=pltpu.HBM)
     block = jax.ShapeDtypeStruct((ROWS, COLS), F32)
     codes = jax.ShapeDtypeStruct((n_dp, ROWS, COLS), bf)
     V = pltpu.VMEM
     dma = pltpu.SemaphoreType.DMA
-    new_master, update, coded, small = pl.pallas_call(
+    row_like, col_like = jax.ShapeDtypeStruct((1, ROWS), F32), jax.ShapeDtypeStruct((COLS,), F32)
+    given = [pltpu.with_memory_space_constraint(a, pltpu.HBM) for a in (grad, master, row_prev, col_prev, history)]
+    new_master, update, coded, row_new, col_new, tail = pl.pallas_call(
         functools.partial(step_kernel, sizes),
-        out_shape=[block, block, codes, jax.ShapeDtypeStruct((16, 128), F32)],
-        in_specs=[anywhere, anywhere, anywhere, anywhere, smem],
-        out_specs=[anywhere, anywhere, anywhere, vmem],
+        out_shape=[block, block, codes, row_like, col_like, jax.ShapeDtypeStruct((8, 128), F32)],
+        in_specs=[hbm] * 5,
+        out_specs=[vmem] * 6,
         scratch_shapes=[
             V((HALF, COLS), bf), V((HALF, COLS), bf),
             V((ROWS, COLS), bf), V((ROWS, COLS), bf), V((ROWS, COLS), bf),
             V((HALF, COLS), bf), V((HALF, COLS), bf), V((HALF, COLS), bf), V((HALF, COLS), bf),
-            V((ROWS, COLS), F32), V((ROWS, COLS), F32), V((ROWS, COLS), F32), V((ROWS, COLS), F32),
-            V((ROWS, COLS), bf), V((ROWS, 128), F32), V((1, 128), F32), V((COLS,), F32),
+            V((ROWS, COLS), F32), V((ROWS, COLS), F32), V((ROWS, 128), F32), V((1, 128), F32), V((COLS,), F32), pltpu.SMEM((16,), F32),
             V((2, 8, 128), F32), V((n_yz, 8, 128), F32),
             V((n_col, 1, 128), F32), V((n_col, 1, 128), F32),
             V((2, 2, 128), F32), V((n_yz, 2, 128), F32),
             V((n_col, 1, 128), F32), V((2, 1, 128), F32), V((n_yz, 1, 128), F32),
-            dma((10,)), dma((10,)), dma((9,)), dma((3,)), dma((3,)), dma((6,)), dma((6,)), dma((6,)), dma((6,)),
+            dma((10,)), dma((10,)), dma((8,)), dma((3,)), dma((3,)), dma((6,)), dma((6,)), dma((6,)), dma((6,)),
         ],
         compiler_params=pltpu.CompilerParams(
             collective_id=0, has_side_effects=True, vmem_limit_bytes=16 * 1024 * 1024
         ),
         name="step",
-    )(grad, master, row_prev, col_prev, history)
+    )(*given)
     new_master, update, row_new, col_new, coded, new_history, row_mean = pl.pallas_call(
         finish_kernel,
         out_shape=[
-            block, block, jax.ShapeDtypeStruct((1, ROWS), F32), jax.ShapeDtypeStruct((COLS,), F32), codes,
+            block, block, row_like, col_like, codes,
             jax.ShapeDtypeStruct((16,), F32), jax.ShapeDtypeStruct((1,), F32),
         ],
-        in_specs=[anywhere, anywhere, anywhere, vmem, smem],
-        out_specs=[anywhere, anywhere, vmem, vmem, anywhere, smem, smem],
-        scratch_shapes=[dma((3,))],
+        in_specs=[anywhere] * 5 + [vmem],
+        out_specs=[hbm] * 7,
+        scratch_shapes=[V((16,), F32), V((1,), F32), dma((7,))],
+        compiler_params=pltpu.CompilerParams(vmem_limit_bytes=1024 * 1024),
         name="finish",
-    )(new_master, update, coded, small, history)
+    )(new_master, update, coded, row_new, col_new, tail)
     return (
         new_master[None], update[None], row_new, col_new, coded, new_history, row_mean.reshape(()),
     )

time: 137 us -> 64.3 us (0.47)
  Pallas kernels: 129 us -> 63.6 us
  local copies, waits for them, and re-layouts: 7.45 us -> 0 us
    pallas_call x1, Pallas kernels: 66.1 us -> 1.38 us  [body(): pl.pallas_call(finish_kernel, out_shape=[block, block, row_like, col_like...]
    unnamed x18 -> x0, local copies, waits for them, and re-layouts: 7.45 us -> none
where the time goes in v2:
time: 64.3 us; the launch traced here: 64.2 us
  Pallas kernels  63.6 us (99%)
    pallas_call x1, Pallas kernels, body(): pl.pallas_call(functools.partial(step_kernel, sizes), out_shape=[block, b...  62.2 us
    pallas_call x1, Pallas kernels, body(): pl.pallas_call(finish_kernel, out_shape=[block, block, row_like, col_like...  1.38 us

profile of v2, /device:TPU:1, one launch (start us, length us, event | category | flops | bytes accessed | tf_op | source)
XLA Modules:
  0.0 64.2 jit_solution(6970976289528628595)
XLA Ops:
  0.6 62.2 %step.1 = (f32[128,1024]{1,0:T(8,128)S(1)}, f32[128,1024]{1,0:T(8,128)S(1)}, bf16[4,128,1024]{2,1,0:T(8,128)(2,1)S(1)}, f32[1,128]{1,0:T(1,128)S(1)}, f32[1024]{0:T(1024)S(1)}, /*index=5*/f32[8,128]{1,0:T(8,128)S(1)}) custom-call(bf16[1,4,128,1024]{3,2,1,0:T(8,128)(2,1)} %grad.1, f32[1,128,1024]{2,1,0:T(8,128)} %master.1, f32[1,128]{1,0:T(1,128)} %row_prev.1, ...), custom_call_target="tpu_custom_call" | custom-call | tf_op jit(solution)/shard_map/step/pallas_call | solution.py:347
  62.8 1.4 %finish.1 = (f32[128,1024]{1,0:T(8,128)}, f32[128,1024]{1,0:T(8,128)}, f32[1,128]{1,0:T(1,128)}, f32[1024]{0:T(1024)}, bf16[4,128,1024]{2,1,0:T(8,128)(2,1)}, /*index=5*/f32[16]{0:T(128)}, f32[1]{0:T(128)}) custom-call(f32[128,1024]{1,0:T(8,128)S(1)} %get-tuple-element.20.nm_in, f32[128,1024]{1,0:T(8,128)S(1)} %get-tuple-element.21.up_in, ...), custom_call_target="tpu_custom_call" | custom-call | tf_op jit(solution)/shard_map/finish/pallas_call | solution.py:368

commit v3 on v2

--- a/solution.py
+++ b/solution.py
@@ -36,7 +36,7 @@
     merge_r, merge_l, from_l, from_r, own, next_own, prev_own, sum_r, sum_l,
     g_buf, m_buf, rowp, rm_buf, cm_buf, old,
     core_c, yz_c, xz_r, xz_t, core_s, yz_s, xz_m, core_m, yz_m,
-    rs_send, rs_recv, loc, core_send, core_recv, grp_send, grp_recv, ag_send, ag_recv,
+    rs_send, rs_recv, loc, core_send, core_recv, grp_send, grp_recv, ag_send, ag_recv, greet,
 ):
     n_dp, n_row, n_col = sizes
     n_zl = n_row // 2
@@ -63,7 +63,14 @@
         for j in far_first(n_x)
         if i or j
     ]
-    contacts = [*yz_peers, mate, *xz_peers]
+    z_near = [
+        (d, r, lax.rem(zh + i, n_zh) * n_x + x) for i in sorted({1 % n_zh, n_zh - 1} - {0})
+    ]
+    near = [(lax.rem(d + i, n_dp), r, c) for i in far_first(n_dp) if i]
+    near += [(d, lax.rem(zl + j, n_zl) * 2 + core, c) for j in far_first(n_zl) if j]
+    near += [(d, r, zh * n_x + lax.rem(x + j, n_x)) for j in far_first(n_x) if j]
+    near += z_near
+    contacts = [*near, mate]
 
     def remote(src, dst, send, recv, to):
         return pltpu.make_async_remote_copy(
@@ -106,6 +113,8 @@
     )
     plain_r.start()
     plain_l.start()
+    for p in near:
+        pl.semaphore_signal(greet.at[0], inc=1, device_id=p, device_id_type=MESH)
     loads[1].wait()
     loads[2].wait()
     merged = []
@@ -122,6 +131,9 @@
         n.start()
         merged.append((m, n))
 
+    pl.semaphore_wait(greet.at[0], len(near))
+    for p in z_near:
+        pl.semaphore_signal(greet.at[1], inc=1, device_id=p, device_id_type=MESH)
     loads[0].wait()
     plain_r.wait_recv()
     plain_l.wait_recv()
@@ -170,6 +182,8 @@
         return jnp.broadcast_to(values, (128, 128)).T
 
     xz_r[c] = lanes_to_row(rowp[...])
+    if z_near:
+        pl.semaphore_wait(greet.at[1], len(z_near))
     group_start(xz_r, c, xz_peers, 0)
     core_c_copy.wait_recv()
     yz_c[q] = core_c[0] + core_c[1]
@@ -359,6 +373,7 @@
             V((2, 2, 128), F32), V((n_yz, 2, 128), F32),
             V((n_col, 1, 128), F32), V((2, 1, 128), F32), V((n_yz, 1, 128), F32),
             dma((10,)), dma((10,)), dma((8,)), dma((3,)), dma((3,)), dma((6,)), dma((6,)), dma((6,)), dma((6,)),
+            pltpu.SemaphoreType.REGULAR((2,)),
         ],
         compiler_params=pltpu.CompilerParams(
             collective_id=0, has_side_effects=True, vmem_limit_bytes=16 * 1024 * 1024

time: 64.3 us -> 59.8 us (0.930)
  Pallas kernels: 63.6 us -> 59 us
    pallas_call x1, Pallas kernels: 62.2 us -> 57.7 us  [body(): pl.pallas_call(functools.partial(step_kernel, sizes), out_shape=[block, b...]
where the time goes in v3:
time: 59.8 us; the launch traced here: 59.7 us
  Pallas kernels  59 us (99%)
  between operations  0.64 us (1%)
    pallas_call x1, Pallas kernels, body(): pl.pallas_call(functools.partial(step_kernel, sizes), out_shape=[block, b...  57.7 us
    pallas_call x1, Pallas kernels, body(): pl.pallas_call(finish_kernel, out_shape=[block, block, row_like, col_like...  1.38 us

profile of v3, /device:TPU:1, one launch (start us, length us, event | category | flops | bytes accessed | tf_op | source)
XLA Modules:
  0.0 59.7 jit_solution(6070422090501976152)
XLA Ops:
  0.6 57.7 %step.1 = (f32[128,1024]{1,0:T(8,128)S(1)}, f32[128,1024]{1,0:T(8,128)S(1)}, bf16[4,128,1024]{2,1,0:T(8,128)(2,1)S(1)}, f32[1,128]{1,0:T(1,128)S(1)}, f32[1024]{0:T(1024)S(1)}, /*index=5*/f32[8,128]{1,0:T(8,128)S(1)}) custom-call(bf16[1,4,128,1024]{3,2,1,0:T(8,128)(2,1)} %grad.1, f32[1,128,1024]{2,1,0:T(8,128)} %master.1, f32[1,128]{1,0:T(1,128)} %row_prev.1, ...), custom_call_target="tpu_custom_call" | custom-call | tf_op jit(solution)/shard_map/step/pallas_call | solution.py:361
  58.3 1.4 %finish.1 = (f32[128,1024]{1,0:T(8,128)}, f32[128,1024]{1,0:T(8,128)}, f32[1,128]{1,0:T(1,128)}, f32[1024]{0:T(1024)}, bf16[4,128,1024]{2,1,0:T(8,128)(2,1)}, /*index=5*/f32[16]{0:T(128)}, f32[1]{0:T(128)}) custom-call(f32[128,1024]{1,0:T(8,128)S(1)} %get-tuple-element.20.nm_in, f32[128,1024]{1,0:T(8,128)S(1)} %get-tuple-element.21.up_in, ...), custom_call_target="tpu_custom_call" | custom-call | tf_op jit(solution)/shard_map/finish/pallas_call | solution.py:383

commit v4 on v3

--- a/solution.py
+++ b/solution.py
@@ -35,7 +35,7 @@
     nm_out, up_out, codes_out, row_out, col_out, tail_out,
     merge_r, merge_l, from_l, from_r, own, next_own, prev_own, sum_r, sum_l,
     g_buf, m_buf, rowp, rm_buf, cm_buf, old,
-    core_c, yz_c, xz_r, xz_t, core_s, yz_s, xz_m, core_m, yz_m,
+    core_c, yz_c, xz_r, xz_t, core_s, yz_s, z_m, core_m, xy_m,
     rs_send, rs_recv, loc, core_send, core_recv, grp_send, grp_recv, ag_send, ag_recv, greet,
 ):
     n_dp, n_row, n_col = sizes
@@ -71,6 +71,19 @@
     near += [(d, r, zh * n_x + lax.rem(x + j, n_x)) for j in far_first(n_x) if j]
     near += z_near
     contacts = [*near, mate]
+    z_peers = [
+        (d, lax.rem(zl + j, n_zl) * 2 + core, lax.rem(zh + i, n_zh) * n_x + x)
+        for i in far_first(n_zh)
+        for j in far_first(n_zl)
+        if i or j
+    ]
+    xy_peers = [
+        (lax.rem(d + i, n_dp), r, zh * n_x + lax.rem(x + j, n_x))
+        for i in far_first(n_dp)
+        for j in far_first(n_x)
+        if i or j
+    ]
+    z_mine, xy_mine = zh * n_zl + zl, d * n_x + x
 
     def remote(src, dst, send, recv, to):
         return pltpu.make_async_remote_copy(
@@ -247,10 +260,14 @@
         new_master = m_buf[:, cols] - learn_rate * update
         up_out[:, cols] = update
         nm_out[:, cols] = new_master
-        codes_out[d, :, cols] = jnp.clip(new_master * scale, -code_limit, code_limit).astype(jnp.bfloat16)
         largest = jnp.maximum(largest, jnp.abs(new_master))
-    xz_m[c] = jnp.max(largest, axis=0, keepdims=True)
-    group_start(xz_m, c, xz_peers, 4)
+    core_m[0] = jnp.max(largest, axis=0, keepdims=True)
+    core_m_copy = remote(core_m.at[0], core_m.at[1], core_send.at[2], core_recv.at[2], mate)
+    core_m_copy.start()
+    codes_out[d] = jnp.clip(nm_out[...] * scale[:, 0:1], -code_limit, code_limit).astype(jnp.bfloat16)
+    core_m_copy.wait_recv()
+    z_m[z_mine] = jnp.maximum(core_m[0], core_m[1])
+    group_start(z_m, z_mine, z_peers, 4)
 
     top, bottom = pl.ds(0, HALF), pl.ds(HALF, HALF)
     to_right = [
@@ -281,13 +298,9 @@
             total = jnp.maximum(total, buf[k])
         return total
 
-    group_wait(xz_m, xz_peers, 4)
-    core_m[0] = max_all(xz_m, n_col)
-    core_m_copy = remote(core_m.at[0], core_m.at[1], core_send.at[2], core_recv.at[2], mate)
-    core_m_copy.start()
-    core_m_copy.wait_recv()
-    yz_m[q] = jnp.maximum(core_m[0], core_m[1])
-    group_start(yz_m, q, yz_peers, 5)
+    group_wait(z_m, z_peers, 4)
+    xy_m[xy_mine] = max_all(z_m, len(z_peers) + 1)
+    group_start(xy_m, xy_mine, xy_peers, 5)
 
     for a, b in first:
         a.wait_send()
@@ -304,17 +317,17 @@
     group_done(yz_c, yz_peers, 1)
     group_done(xz_t, xz_peers, 2)
     group_done(yz_s, yz_peers, 3)
-    group_done(xz_m, xz_peers, 4)
+    group_done(z_m, z_peers, 4)
     to_right[1].wait_recv()
     to_left[1].wait_recv()
     on_right.wait_recv()
     on_left.wait_recv()
-    group_wait(yz_m, yz_peers, 5)
-    newest = jnp.max(max_all(yz_m, n_yz), axis=1, keepdims=True)
+    group_wait(xy_m, xy_peers, 5)
+    newest = jnp.max(max_all(xy_m, len(xy_peers) + 1), axis=1, keepdims=True)
     tail_out[0:1] = jnp.where(lane == 15, newest, shifted)
     for cp in (*to_right, *to_left, on_right, on_left):
         cp.wait_send()
-    group_done(yz_m, yz_peers, 5)
+    group_done(xy_m, xy_peers, 5)
 
 
 def finish_kernel(
@@ -348,6 +361,7 @@
 def body(sizes, grad, master, row_prev, col_prev, history):
     n_dp, n_row, n_col = sizes
     n_yz = n_dp * n_row // 2
+    n_x = min(n_col, 4)
     bf = jnp.bfloat16
     anywhere = pl.BlockSpec(memory_space=pl.ANY)
     vmem = pl.BlockSpec(memory_space=pltpu.VMEM)
@@ -371,7 +385,7 @@
             V((2, 8, 128), F32), V((n_yz, 8, 128), F32),
             V((n_col, 1, 128), F32), V((n_col, 1, 128), F32),
             V((2, 2, 128), F32), V((n_yz, 2, 128), F32),
-            V((n_col, 1, 128), F32), V((2, 1, 128), F32), V((n_yz, 1, 128), F32),
+            V((n_col // n_x * n_row // 2, 1, 128), F32), V((2, 1, 128), F32), V((n_dp * n_x, 1, 128), F32),
             dma((10,)), dma((10,)), dma((8,)), dma((3,)), dma((3,)), dma((6,)), dma((6,)), dma((6,)), dma((6,)),
             pltpu.SemaphoreType.REGULAR((2,)),
         ],

time: 59.8 us -> 59.3 us (level)
  no operation moved by 1% of the time
where the time goes in v4:
time: 59.3 us; the launch traced here: 59.2 us
  Pallas kernels  58.6 us (99%)
  between operations  0.64 us (1%)
    pallas_call x1, Pallas kernels, body(): pl.pallas_call(functools.partial(step_kernel, sizes), out_shape=[block, b...  57.2 us
    pallas_call x1, Pallas kernels, body(): pl.pallas_call(finish_kernel, out_shape=[block, block, row_like, col_like...  1.38 us

profile of v4, /device:TPU:1, one launch (start us, length us, event | category | flops | bytes accessed | tf_op | source)
XLA Modules:
  0.0 59.2 jit_solution(8015744967255978262)
XLA Ops:
  0.6 57.2 %step.1 = (f32[128,1024]{1,0:T(8,128)S(1)}, f32[128,1024]{1,0:T(8,128)S(1)}, bf16[4,128,1024]{2,1,0:T(8,128)(2,1)S(1)}, f32[1,128]{1,0:T(1,128)S(1)}, f32[1024]{0:T(1024)S(1)}, /*index=5*/f32[8,128]{1,0:T(8,128)S(1)}) custom-call(bf16[1,4,128,1024]{3,2,1,0:T(8,128)(2,1)} %grad.1, f32[1,128,1024]{2,1,0:T(8,128)} %master.1, f32[1,128]{1,0:T(1,128)} %row_prev.1, ...), custom_call_target="tpu_custom_call" | custom-call | tf_op jit(solution)/shard_map/step/pallas_call | solution.py:375
  57.8 1.4 %finish.1 = (f32[128,1024]{1,0:T(8,128)}, f32[128,1024]{1,0:T(8,128)}, f32[1,128]{1,0:T(1,128)}, f32[1024]{0:T(1024)}, bf16[4,128,1024]{2,1,0:T(8,128)(2,1)}, /*index=5*/f32[16]{0:T(128)}, f32[1]{0:T(128)}) custom-call(f32[128,1024]{1,0:T(8,128)S(1)} %get-tuple-element.20.nm_in, f32[128,1024]{1,0:T(8,128)S(1)} %get-tuple-element.21.up_in, ...), custom_call_target="tpu_custom_call" | custom-call | tf_op jit(solution)/shard_map/finish/pallas_call | solution.py:397

commit v5 on v4

--- a/solution.py
+++ b/solution.py
@@ -19,6 +19,8 @@
 ROWS, COLS = 128, 1024
 HALF = ROWS // 2
 CHUNK = 32
+EARLY = 64
+LATE = ROWS - EARLY
 TILES = COLS // 128
 
 
@@ -36,7 +38,7 @@
     merge_r, merge_l, from_l, from_r, own, next_own, prev_own, sum_r, sum_l,
     g_buf, m_buf, rowp, rm_buf, cm_buf, old,
     core_c, yz_c, xz_r, xz_t, core_s, yz_s, z_m, core_m, xy_m,
-    rs_send, rs_recv, loc, core_send, core_recv, grp_send, grp_recv, ag_send, ag_recv, greet,
+    rs_send, rs_recv, loc, core_send, core_recv, grp_send, grp_recv, ag_send, ag_recv, greet, masters, steps,
 ):
     n_dp, n_row, n_col = sizes
     n_zl = n_row // 2
@@ -83,6 +85,7 @@
         for j in far_first(n_x)
         if i or j
     ]
+    dp_peers = [(lax.rem(d + i, n_dp), r, c) for i in far_first(n_dp) if i]
     z_mine, xy_mine = zh * n_zl + zl, d * n_x + x
 
     def remote(src, dst, send, recv, to):
@@ -128,6 +131,8 @@
     plain_l.start()
     for p in near:
         pl.semaphore_signal(greet.at[0], inc=1, device_id=p, device_id_type=MESH)
+    loads[3].wait()
+    masters[d] = m_buf[pl.ds(LATE, EARLY)].astype(jnp.bfloat16)
     loads[1].wait()
     loads[2].wait()
     merged = []
@@ -182,6 +187,16 @@
     def group_done(buf, peers, i):
         whole_wait(buf.at[pl.ds(0, len(peers))], grp_send.at[i])
 
+    def block_start(buf, i):
+        for p in dp_peers:
+            remote(buf.at[d], buf.at[d], ag_send.at[i], ag_recv.at[i], p).start()
+
+    def block_wait(i):
+        whole_wait(masters.at[pl.ds(0, n_dp - 1)], ag_recv.at[i])
+
+    def block_done(i):
+        whole_wait(masters.at[pl.ds(0, n_dp - 1)], ag_send.at[i])
+
     def add_all(buf, n):
         total = buf[0]
         for k in range(1, n):
@@ -201,6 +216,7 @@
     core_c_copy.wait_recv()
     yz_c[q] = core_c[0] + core_c[1]
     group_start(yz_c, q, yz_peers, 1)
+    block_start(masters, 0)
     loads[4].wait()
     loads[5].wait()
     group_wait(yz_c, yz_peers, 1)
@@ -225,6 +241,12 @@
     row_new = decay_rate * rm_buf[...] + (1.0 - decay_rate) * (row_total / total_cols)
     row_out[...] = row_new
     row_factor = row_to_lanes(1.0 / jnp.sqrt(row_new))
+    for k in range(TILES):
+        cols = pl.ds(128 * k, 128)
+        step = g_buf[:, cols] * row_factor * root_col[k : k + 1]
+        g_buf[:, cols] = step
+        steps[d, :, cols] = step[LATE:].astype(jnp.bfloat16)
+    block_start(steps, 1)
     group_wait(xz_t, xz_peers, 2)
     weighted = add_all(xz_t, n_col) / row_new
 
@@ -243,7 +265,6 @@
     for i in range(15):
         shifted = jnp.where(lane == i, old[i + 1], shifted)
     scale = code_limit / jnp.full((1, 128), largest_old, F32)
-    loads[3].wait()
     group_wait(yz_s, yz_peers, 3)
     totals = jnp.sum(add_all(yz_s, n_yz), axis=1, keepdims=True)
     row_mean = totals[1:2] / total_rows
@@ -251,12 +272,11 @@
     factor = jnp.sqrt(row_mean) / jnp.maximum(1.0, step_rms / clip_limit)
     tail_out[1:2] = jnp.broadcast_to(row_mean, (1, 128))
     tail_out[2:8] = jnp.zeros((6, 128), F32)
-    row_factor = row_factor * factor
 
     largest = jnp.zeros((ROWS, 128), F32)
     for k in range(TILES):
         cols = pl.ds(128 * k, 128)
-        update = g_buf[:, cols] * row_factor * root_col[k : k + 1]
+        update = g_buf[:, cols] * factor
         new_master = m_buf[:, cols] - learn_rate * update
         up_out[:, cols] = update
         nm_out[:, cols] = new_master
@@ -264,31 +284,40 @@
     core_m[0] = jnp.max(largest, axis=0, keepdims=True)
     core_m_copy = remote(core_m.at[0], core_m.at[1], core_send.at[2], core_recv.at[2], mate)
     core_m_copy.start()
-    codes_out[d] = jnp.clip(nm_out[...] * scale[:, 0:1], -code_limit, code_limit).astype(jnp.bfloat16)
     core_m_copy.wait_recv()
     z_m[z_mine] = jnp.maximum(core_m[0], core_m[1])
     group_start(z_m, z_mine, z_peers, 4)
 
-    top, bottom = pl.ds(0, HALF), pl.ds(HALF, HALF)
+    top, bottom = pl.ds(0, LATE // 2), pl.ds(LATE // 2, LATE // 2)
+    codes_out[d, pl.ds(0, LATE)] = jnp.clip(nm_out[pl.ds(0, LATE)] * scale[:, 0:1], -code_limit, code_limit).astype(
+        jnp.bfloat16
+    )
     to_right = [
-        remote(codes_out.at[d, part], codes_out.at[d, part], ag_send.at[i], ag_recv.at[i], right)
+        remote(codes_out.at[d, part], codes_out.at[d, part], ag_send.at[2 + i], ag_recv.at[2 + i], right)
         for i, part in enumerate((top, bottom))
     ]
     to_left = [
-        remote(codes_out.at[d, part], codes_out.at[d, part], ag_send.at[2 + i], ag_recv.at[2 + i], left)
+        remote(codes_out.at[d, part], codes_out.at[d, part], ag_send.at[4 + i], ag_recv.at[4 + i], left)
         for i, part in enumerate((bottom, top))
     ]
     for i in range(2):
         to_right[i].start()
         to_left[i].start()
+
+    block_wait(0)
+    block_wait(1)
+    rate = learn_rate * factor
+    for j in range(n_dp):
+        moved = masters[j].astype(F32) - rate * steps[j].astype(F32)
+        codes_out[j, pl.ds(LATE, EARLY)] = jnp.clip(moved * scale[:, 0:1], -code_limit, code_limit).astype(jnp.bfloat16)
     to_right[0].wait_recv()
     on_right = remote(
-        codes_out.at[dp_, top], codes_out.at[dp_, top], ag_send.at[4], ag_recv.at[4], right
+        codes_out.at[dp_, top], codes_out.at[dp_, top], ag_send.at[6], ag_recv.at[6], right
     )
     on_right.start()
     to_left[0].wait_recv()
     on_left = remote(
-        codes_out.at[dn, bottom], codes_out.at[dn, bottom], ag_send.at[5], ag_recv.at[5], left
+        codes_out.at[dn, bottom], codes_out.at[dn, bottom], ag_send.at[7], ag_recv.at[7], left
     )
     on_left.start()
 
@@ -327,6 +356,8 @@
     tail_out[0:1] = jnp.where(lane == 15, newest, shifted)
     for cp in (*to_right, *to_left, on_right, on_left):
         cp.wait_send()
+    block_done(0)
+    block_done(1)
     group_done(xy_m, xy_peers, 5)
 
 
@@ -386,8 +417,8 @@
             V((n_col, 1, 128), F32), V((n_col, 1, 128), F32),
             V((2, 2, 128), F32), V((n_yz, 2, 128), F32),
             V((n_col // n_x * n_row // 2, 1, 128), F32), V((2, 1, 128), F32), V((n_dp * n_x, 1, 128), F32),
-            dma((10,)), dma((10,)), dma((8,)), dma((3,)), dma((3,)), dma((6,)), dma((6,)), dma((6,)), dma((6,)),
-            pltpu.SemaphoreType.REGULAR((2,)),
+            dma((10,)), dma((10,)), dma((8,)), dma((3,)), dma((3,)), dma((6,)), dma((6,)), dma((8,)), dma((8,)),
+            pltpu.SemaphoreType.REGULAR((2,)), V((n_dp, EARLY, COLS), bf), V((n_dp, EARLY, COLS), bf),
         ],
         compiler_params=pltpu.CompilerParams(
             collective_id=0, has_side_effects=True, vmem_limit_bytes=16 * 1024 * 1024

time: 59.3 us -> 57.6 us (0.971)
  Pallas kernels: 58.6 us -> 56.8 us
    pallas_call x1, Pallas kernels: 57.2 us -> 55.4 us  [body(): pl.pallas_call(functools.partial(step_kernel, sizes), out_shape=[block, b...]
where the time goes in v5:
time: 57.6 us; the launch traced here: 57.4 us
  Pallas kernels  56.8 us (99%)
  between operations  0.64 us (1%)
    pallas_call x1, Pallas kernels, body(): pl.pallas_call(functools.partial(step_kernel, sizes), out_shape=[block, b...  55.4 us
    pallas_call x1, Pallas kernels, body(): pl.pallas_call(finish_kernel, out_shape=[block, block, row_like, col_like...  1.38 us

profile of v5, /device:TPU:1, one launch (start us, length us, event | category | flops | bytes accessed | tf_op | source)
XLA Modules:
  0.0 57.4 jit_solution(1937842630311166127)
XLA Ops:
  0.6 55.4 %step.1 = (f32[128,1024]{1,0:T(8,128)S(1)}, f32[128,1024]{1,0:T(8,128)S(1)}, bf16[4,128,1024]{2,1,0:T(8,128)(2,1)S(1)}, f32[1,128]{1,0:T(1,128)S(1)}, f32[1024]{0:T(1024)S(1)}, /*index=5*/f32[8,128]{1,0:T(8,128)S(1)}) custom-call(bf16[1,4,128,1024]{3,2,1,0:T(8,128)(2,1)} %grad.1, f32[1,128,1024]{2,1,0:T(8,128)} %master.1, f32[1,128]{1,0:T(1,128)} %row_prev.1, ...), custom_call_target="tpu_custom_call" | custom-call | tf_op jit(solution)/shard_map/step/pallas_call | solution.py:406
  56.1 1.4 %finish.1 = (f32[128,1024]{1,0:T(8,128)}, f32[128,1024]{1,0:T(8,128)}, f32[1,128]{1,0:T(1,128)}, f32[1024]{0:T(1024)}, bf16[4,128,1024]{2,1,0:T(8,128)(2,1)}, /*index=5*/f32[16]{0:T(128)}, f32[1]{0:T(128)}) custom-call(f32[128,1024]{1,0:T(8,128)S(1)} %get-tuple-element.20.nm_in, f32[128,1024]{1,0:T(8,128)S(1)} %get-tuple-element.21.up_in, ...), custom_call_target="tpu_custom_call" | custom-call | tf_op jit(solution)/shard_map/finish/pallas_call | solution.py:428

commit v6 on v5

--- a/solution.py
+++ b/solution.py
@@ -273,17 +273,19 @@
     tail_out[1:2] = jnp.broadcast_to(row_mean, (1, 128))
     tail_out[2:8] = jnp.zeros((6, 128), F32)
 
+    rate = learn_rate * factor
     largest = jnp.zeros((ROWS, 128), F32)
     for k in range(TILES):
         cols = pl.ds(128 * k, 128)
-        update = g_buf[:, cols] * factor
-        new_master = m_buf[:, cols] - learn_rate * update
-        up_out[:, cols] = update
-        nm_out[:, cols] = new_master
-        largest = jnp.maximum(largest, jnp.abs(new_master))
+        largest = jnp.maximum(largest, jnp.abs(m_buf[:, cols] - rate * g_buf[:, cols]))
     core_m[0] = jnp.max(largest, axis=0, keepdims=True)
     core_m_copy = remote(core_m.at[0], core_m.at[1], core_send.at[2], core_recv.at[2], mate)
     core_m_copy.start()
+    for k in range(TILES):
+        cols = pl.ds(128 * k, 128)
+        update = g_buf[:, cols] * factor
+        up_out[:, cols] = update
+        nm_out[:, cols] = m_buf[:, cols] - learn_rate * update
     core_m_copy.wait_recv()
     z_m[z_mine] = jnp.maximum(core_m[0], core_m[1])
     group_start(z_m, z_mine, z_peers, 4)
@@ -304,12 +306,6 @@
         to_right[i].start()
         to_left[i].start()
 
-    block_wait(0)
-    block_wait(1)
-    rate = learn_rate * factor
-    for j in range(n_dp):
-        moved = masters[j].astype(F32) - rate * steps[j].astype(F32)
-        codes_out[j, pl.ds(LATE, EARLY)] = jnp.clip(moved * scale[:, 0:1], -code_limit, code_limit).astype(jnp.bfloat16)
     to_right[0].wait_recv()
     on_right = remote(
         codes_out.at[dp_, top], codes_out.at[dp_, top], ag_send.at[6], ag_recv.at[6], right
@@ -330,6 +326,12 @@
     group_wait(z_m, z_peers, 4)
     xy_m[xy_mine] = max_all(z_m, len(z_peers) + 1)
     group_start(xy_m, xy_mine, xy_peers, 5)
+
+    block_wait(0)
+    block_wait(1)
+    for j in range(n_dp):
+        moved = masters[j].astype(F32) - rate * steps[j].astype(F32)
+        codes_out[j, pl.ds(LATE, EARLY)] = jnp.clip(moved * scale[:, 0:1], -code_limit, code_limit).astype(jnp.bfloat16)
 
     for a, b in first:
         a.wait_send()

time: 57.6 us -> 57.4 us (level)
  no operation moved by 1% of the time
where the time goes in v6:
time: 57.4 us; the launch traced here: 57.3 us
  Pallas kernels  56.6 us (99%)
  between operations  0.64 us (1%)
    pallas_call x1, Pallas kernels, body(): pl.pallas_call(functools.partial(step_kernel, sizes), out_shape=[block, b...  55.3 us
    pallas_call x1, Pallas kernels, body(): pl.pallas_call(finish_kernel, out_shape=[block, block, row_like, col_like...  1.38 us

profile of v6, /device:TPU:1, one launch (start us, length us, event | category | flops | bytes accessed | tf_op | source)
XLA Modules:
  0.0 57.3 jit_solution(15676169133144025982)
XLA Ops:
  0.6 55.3 %step.1 = (f32[128,1024]{1,0:T(8,128)S(1)}, f32[128,1024]{1,0:T(8,128)S(1)}, bf16[4,128,1024]{2,1,0:T(8,128)(2,1)S(1)}, f32[1,128]{1,0:T(1,128)S(1)}, f32[1024]{0:T(1024)S(1)}, /*index=5*/f32[8,128]{1,0:T(8,128)S(1)}) custom-call(bf16[1,4,128,1024]{3,2,1,0:T(8,128)(2,1)} %grad.1, f32[1,128,1024]{2,1,0:T(8,128)} %master.1, f32[1,128]{1,0:T(1,128)} %row_prev.1, ...), custom_call_target="tpu_custom_call" | custom-call | tf_op jit(solution)/shard_map/step/pallas_call | solution.py:408
  55.9 1.4 %finish.1 = (f32[128,1024]{1,0:T(8,128)}, f32[128,1024]{1,0:T(8,128)}, f32[1,128]{1,0:T(1,128)}, f32[1024]{0:T(1024)}, bf16[4,128,1024]{2,1,0:T(8,128)(2,1)}, /*index=5*/f32[16]{0:T(128)}, f32[1]{0:T(128)}) custom-call(f32[128,1024]{1,0:T(8,128)S(1)} %get-tuple-element.20.nm_in, f32[128,1024]{1,0:T(8,128)S(1)} %get-tuple-element.21.up_in, ...), custom_call_target="tpu_custom_call" | custom-call | tf_op jit(solution)/shard_map/finish/pallas_call | solution.py:430

commit v7 on v6

--- a/solution.py
+++ b/solution.py
@@ -85,6 +85,14 @@
         for j in far_first(n_x)
         if i or j
     ]
+    xzc_peers = [
+        (d, zl * 2 + lax.rem(core + k, 2), lax.rem(zh + i, n_zh) * n_x + lax.rem(x + j, n_x))
+        for i in far_first(n_zh)
+        for j in far_first(n_x)
+        for k in range(2)
+        if i or j or k
+    ]
+    xzc_mine = c * 2 + core
     dp_peers = [(lax.rem(d + i, n_dp), r, c) for i in far_first(n_dp) if i]
     z_mine, xy_mine = zh * n_zl + zl, d * n_x + x
 
@@ -213,6 +221,7 @@
     if z_near:
         pl.semaphore_wait(greet.at[1], len(z_near))
     group_start(xz_r, c, xz_peers, 0)
+    pl.semaphore_signal(greet.at[2], inc=1, device_id=mate, device_id_type=MESH)
     core_c_copy.wait_recv()
     yz_c[q] = core_c[0] + core_c[1]
     group_start(yz_c, q, yz_peers, 1)
@@ -234,12 +243,16 @@
     for k in range(TILES):
         g = g_buf[:, pl.ds(128 * k, 128)]
         lanes = lanes + g * g * inv_col[k : k + 1]
-    xz_t[c] = lanes_to_row(lanes)
-    group_start(xz_t, c, xz_peers, 2)
+    pl.semaphore_wait(greet.at[2], 1)
+    xz_t[xzc_mine] = lanes_to_row(lanes)
+    group_start(xz_t, xzc_mine, xzc_peers, 2)
     group_wait(xz_r, xz_peers, 0)
     row_total = add_all(xz_r, n_col)
     row_new = decay_rate * rm_buf[...] + (1.0 - decay_rate) * (row_total / total_cols)
     row_out[...] = row_new
+    core_s[0] = row_new
+    core_s_copy = remote(core_s.at[0], core_s.at[1], core_send.at[1], core_recv.at[1], mate)
+    core_s_copy.start()
     row_factor = row_to_lanes(1.0 / jnp.sqrt(row_new))
     for k in range(TILES):
         cols = pl.ds(128 * k, 128)
@@ -247,14 +260,17 @@
         g_buf[:, cols] = step
         steps[d, :, cols] = step[LATE:].astype(jnp.bfloat16)
     block_start(steps, 1)
-    group_wait(xz_t, xz_peers, 2)
-    weighted = add_all(xz_t, n_col) / row_new
-
-    core_s[0] = jnp.concatenate([weighted, row_new], axis=0)
-    core_s_copy = remote(core_s.at[0], core_s.at[1], core_send.at[1], core_recv.at[1], mate)
-    core_s_copy.start()
     core_s_copy.wait_recv()
-    yz_s[q] = core_s[0] + core_s[1]
+    row_first = jnp.where(core == 0, row_new, core_s[1])
+    row_second = jnp.where(core == 0, core_s[1], row_new)
+    group_wait(xz_t, xzc_peers, 2)
+    first_total, second_total = xz_t[0], xz_t[1]
+    for k in range(1, n_col):
+        first_total = first_total + xz_t[2 * k]
+        second_total = second_total + xz_t[2 * k + 1]
+    weighted = first_total / row_first + second_total / row_second
+
+    yz_s[q] = jnp.concatenate([weighted, row_first + row_second], axis=0)
     group_start(yz_s, q, yz_peers, 3)
     loads[6].wait()
     largest_old = old[0]
@@ -346,7 +362,7 @@
     core_m_copy.wait_send()
     group_done(xz_r, xz_peers, 0)
     group_done(yz_c, yz_peers, 1)
-    group_done(xz_t, xz_peers, 2)
+    group_done(xz_t, xzc_peers, 2)
     group_done(yz_s, yz_peers, 3)
     group_done(z_m, z_peers, 4)
     to_right[1].wait_recv()
@@ -416,11 +432,11 @@
             V((HALF, COLS), bf), V((HALF, COLS), bf), V((HALF, COLS), bf), V((HALF, COLS), bf),
             V((ROWS, COLS), F32), V((ROWS, COLS), F32), V((ROWS, 128), F32), V((1, 128), F32), V((COLS,), F32), pltpu.SMEM((16,), F32),
             V((2, 8, 128), F32), V((n_yz, 8, 128), F32),
-            V((n_col, 1, 128), F32), V((n_col, 1, 128), F32),
-            V((2, 2, 128), F32), V((n_yz, 2, 128), F32),
+            V((n_col, 1, 128), F32), V((2 * n_col, 1, 128), F32),
+            V((2, 1, 128), F32), V((n_yz, 2, 128), F32),
             V((n_col // n_x * n_row // 2, 1, 128), F32), V((2, 1, 128), F32), V((n_dp * n_x, 1, 128), F32),
             dma((10,)), dma((10,)), dma((8,)), dma((3,)), dma((3,)), dma((6,)), dma((6,)), dma((8,)), dma((8,)),
-            pltpu.SemaphoreType.REGULAR((2,)), V((n_dp, EARLY, COLS), bf), V((n_dp, EARLY, COLS), bf),
+            pltpu.SemaphoreType.REGULAR((3,)), V((n_dp, EARLY, COLS), bf), V((n_dp, EARLY, COLS), bf),
         ],
         compiler_params=pltpu.CompilerParams(
             collective_id=0, has_side_effects=True, vmem_limit_bytes=16 * 1024 * 1024

time: 57.4 us -> 57.2 us (level)
  no operation moved by 1% of the time
where the time goes in v7:
time: 57.2 us; the launch traced here: 57.1 us
  Pallas kernels  56.5 us (99%)
  between operations  0.64 us (1%)
    pallas_call x1, Pallas kernels, body(): pl.pallas_call(functools.partial(step_kernel, sizes), out_shape=[block, b...  55.1 us
    pallas_call x1, Pallas kernels, body(): pl.pallas_call(finish_kernel, out_shape=[block, block, row_like, col_like...  1.38 us

profile of v7, /device:TPU:1, one launch (start us, length us, event | category | flops | bytes accessed | tf_op | source)
XLA Modules:
  0.0 57.1 jit_solution(15057877037585304409)
XLA Ops:
  0.6 55.1 %step.1 = (f32[128,1024]{1,0:T(8,128)S(1)}, f32[128,1024]{1,0:T(8,128)S(1)}, bf16[4,128,1024]{2,1,0:T(8,128)(2,1)S(1)}, f32[1,128]{1,0:T(1,128)S(1)}, f32[1024]{0:T(1024)S(1)}, /*index=5*/f32[8,128]{1,0:T(8,128)S(1)}) custom-call(bf16[1,4,128,1024]{3,2,1,0:T(8,128)(2,1)} %grad.1, f32[1,128,1024]{2,1,0:T(8,128)} %master.1, f32[1,128]{1,0:T(1,128)} %row_prev.1, ...), custom_call_target="tpu_custom_call" | custom-call | tf_op jit(solution)/shard_map/step/pallas_call | solution.py:424
  55.7 1.4 %finish.1 = (f32[128,1024]{1,0:T(8,128)}, f32[128,1024]{1,0:T(8,128)}, f32[1,128]{1,0:T(1,128)}, f32[1024]{0:T(1024)}, bf16[4,128,1024]{2,1,0:T(8,128)(2,1)}, /*index=5*/f32[16]{0:T(128)}, f32[1]{0:T(128)}) custom-call(f32[128,1024]{1,0:T(8,128)S(1)} %get-tuple-element.20.nm_in, f32[128,1024]{1,0:T(8,128)S(1)} %get-tuple-element.21.up_in, ...), custom_call_target="tpu_custom_call" | custom-call | tf_op jit(solution)/shard_map/finish/pallas_call | solution.py:446
